TPU v7x, 32 devices: a whole 2x2x4 slice. The times are simulated.
32 devices in a mesh: ep: 16 (over z, y, core), tp: 2 (over x).
Axes of the slice: x: 2, y: 2, z: 4, core: 2. Of those that a mesh axis runs over, the one named last changes fastest.
Arguments:
- tokens: bfloat16 [32, 256, 1280], P('ep', None, 'tp'), may hold values from -400 to 400
- router: bfloat16 [1280, 16], P('tp'), may hold values from -2 to 2
- w_in: bfloat16 [16, 1280, 2560], P('ep', None, 'tp'), may hold values from -0.15625 to 0.15625
- w_out: bfloat16 [16, 2560, 1280], P('ep', 'tp'), may hold values from -0.125 to 0.125
- grad_out: bfloat16 [32, 256, 1280], P('ep', None, 'tp'), may hold values from -6 to 6
Outputs:
- grad_tokens: bfloat16 [32, 256, 1280], P('ep', None, 'tp')
- grad_router: float32 [1280, 16], P('tp')
- grad_w_in: bfloat16 [16, 1280, 2560], P('ep', None, 'tp')
All inputs are finite; a program needn't handle non-finite values.
Results may differ from a plain program's by a relative error of at most 0.0095.
Values may be sent and summed in bfloat16 or wider, within the bound.
A program may use at most 64 MiB of HBM per device.

v0:
```python
from functools import partial

import jax
import jax.numpy as jnp
from jax import lax
from jax.sharding import PartitionSpec as P


def on_device(tokens, router, w_in, w_out, grad_out):
    partial_logits = jnp.einsum("bmd,de->bme", tokens, router, preferred_element_type=jnp.float32)
    logits = lax.psum(partial_logits, "tp")
    dispatch = jax.nn.softmax(logits, axis=1)
    combine = jax.nn.softmax(logits, axis=2)
    dispatch_b = dispatch.astype(jnp.bfloat16)
    combine_b = combine.astype(jnp.bfloat16)
    slot_half = jnp.einsum(
        "bme,bmd->ebd", dispatch_b, tokens, preferred_element_type=jnp.float32
    ).astype(jnp.bfloat16)
    grad_half = jnp.einsum(
        "bme,bmd->ebd", combine_b, grad_out, preferred_element_type=jnp.float32
    ).astype(jnp.bfloat16)
    sent_in, sent_grad = (
        lax.all_to_all(slot_half, "ep", split_axis=0, concat_axis=1, tiled=True),
        lax.all_to_all(grad_half, "ep", split_axis=0, concat_axis=1, tiled=True),
    )
    slot_in, slot_grad = (
        lax.all_gather(sent_in, "tp", axis=2, tiled=True),
        lax.all_gather(sent_grad, "tp", axis=2, tiled=True),
    )
    slot_in = slot_in[0]
    slot_grad = slot_grad[0]
    weight_in = w_in[0]
    weight_out = w_out[0]
    all_rows = slot_in.shape[0]
    pre = jnp.dot(slot_in, weight_in, preferred_element_type=jnp.float32)
    act, back = jax.vjp(partial(jax.nn.gelu, approximate=True), pre)
    out_part = jnp.dot(act.astype(jnp.bfloat16), weight_out, preferred_element_type=jnp.float32)
    out_share = lax.psum_scatter(out_part, "tp", scatter_dimension=1, tiled=True).astype(
        jnp.bfloat16
    )
    slot_out = lax.all_to_all(
        out_share.reshape(1, all_rows, -1), "ep", split_axis=1, concat_axis=0, tiled=True
    )
    act_grad = jnp.einsum("bd,fd->bf", slot_grad, weight_out, preferred_element_type=jnp.float32)
    pre_grad = back(act_grad)[0].astype(jnp.bfloat16)
    grad_weight = jnp.einsum(
        "bd,bf->df", slot_in, pre_grad, preferred_element_type=jnp.float32
    ).astype(jnp.bfloat16)
    in_part = jnp.einsum("bf,df->bd", pre_grad, weight_in, preferred_element_type=jnp.float32)
    in_share = lax.psum_scatter(in_part, "tp", scatter_dimension=1, tiled=True).astype(jnp.bfloat16)
    slot_in_grad = lax.all_to_all(
        in_share.reshape(1, all_rows, -1), "ep", split_axis=1, concat_axis=0, tiled=True
    )
    combine_part = jnp.einsum(
        "bmd,ebd->bme", grad_out, slot_out, preferred_element_type=jnp.float32
    )
    combine_dot = lax.psum(combine_part, "tp")
    dispatch_part = jnp.einsum(
        "bmd,ebd->bme", tokens, slot_in_grad, preferred_element_type=jnp.float32
    )
    dispatch_dot = lax.psum(dispatch_part, "tp")
    logit_grad = combine * (combine_dot - jnp.sum(combine * combine_dot, axis=2, keepdims=True))
    logit_grad = logit_grad + dispatch * (
        dispatch_dot - jnp.sum(dispatch * dispatch_dot, axis=1, keepdims=True)
    )
    logit_b = logit_grad.astype(jnp.bfloat16)
    grad_tokens = jnp.einsum(
        "bme,ebd->bmd", dispatch_b, slot_in_grad, preferred_element_type=jnp.float32
    )
    grad_tokens = grad_tokens + jnp.einsum(
        "bme,de->bmd", logit_b, router, preferred_element_type=jnp.float32
    )
    router_part = jnp.einsum("bmd,bme->de", tokens, logit_b, preferred_element_type=jnp.float32)
    grad_router = lax.psum(router_part, "ep")
    return (
        grad_tokens.astype(jnp.bfloat16),
        grad_router,
        grad_weight.reshape(1, grad_weight.shape[0], grad_weight.shape[1]),
    )


def solution(mesh):
    placed = (
        P("ep", None, "tp"),
        P("tp", None),
        P("ep", None, "tp"),
        P("ep", "tp", None),
        P("ep", None, "tp"),
    )
    return jax.shard_map(
        on_device,
        mesh=mesh,
        in_specs=placed,
        out_specs=(P("ep", None, "tp"), P("tp", None), P("ep", None, "tp")),
        check_vma=False,
    )
```

profile of v0, /device:TPU:0, one launch (start us, length us, event | category | flops | bytes accessed | tf_op | source)
XLA Modules:
  0.0 182.5 jit_solution(10628850386178059703)
XLA Ops:
  7.2 1.5 fusion.52
  8.7 9.9 %psum.28 = f32[2,256,16]{1,2,0:T(8,128)S(1)} all-reduce(f32[2,256,16]{1,2,0:T(8,128)S(1)} %fusion.52), channel_id=1, replica_groups=mesh['ep'=16,'tp'=2] {'tp'}, use_global_device_ids=true, to_apply=%region_0.0 | all-reduce | flops 8192 | bytes 65536 | tf_op jit(solution)/shard_map/psum | solution.py:11
  21.2 5.8 %all-to-all-start = ((bf16[16,2,640]{2,1,0:T(2,128)(2,1)}), bf16[16,2,640]{2,1,0:T(2,128)(2,1)S(1)}, u32[]{:S(2)}, u32[]{:S(2)}) async-start(bf16[16,2,640]{2,1,0:T(2,128)(2,1)} %copy.20), calls=%async_computation | async-start | bytes 81920 | tf_op jit(solution)/shard_map/all_to_all | solution.py:24
  27.7 1.3 fusion.17
  29.7 4.0 %all-to-all-done = bf16[16,2,640]{2,1,0:T(2,128)(2,1)S(1)} async-done(((bf16[16,2,640]{2,1,0:T(2,128)(2,1)}), bf16[16,2,640]{2,1,0:T(2,128)(2,1)S(1)}, u32[]{:S(2)}, u32[]{:S(2)}) %all-to-all-start) | async-done | bytes 40992 | tf_op jit(solution)/shard_map/all_to_all | solution.py:24
  33.7 3.5 %all-to-all-start.1 = ((bf16[16,2,640]{2,1,0:T(2,128)(2,1)}), bf16[16,2,640]{2,1,0:T(2,128)(2,1)S(1)}, u32[]{:S(2)}, u32[]{:S(2)}) async-start(bf16[16,2,640]{2,1,0:T(2,128)(2,1)} %copy.21), calls=%async_computation.1 | async-start | bytes 81920 | tf_op jit(solution)/shard_map/all_to_all | solution.py:23
  37.3 4.8 %all_gather.6 = bf16[1,32,1280]{2,1,0:T(8,128)(2,1)} all-gather(bf16[1,32,640]{2,1,0:T(8,128)(2,1)S(1)} %all_to_all.17), channel_id=1, replica_groups=mesh['ep'=16,'tp'=2] {'tp'}, dimensions={2}, use_global_device_ids=true | all-gather | bytes 122880 | tf_op jit(solution)/shard_map/all_gather | solution.py:28
  42.1 1.8 all-to-all-done.1
  43.9 4.7 %all_gather.7 = bf16[1,32,1280]{2,1,0:T(8,128)(2,1)S(1)} all-gather(bf16[1,32,640]{2,1,0:T(8,128)(2,1)S(1)} %all_to_all.19), channel_id=1, replica_groups=mesh['ep'=16,'tp'=2] {'tp'}, dimensions={2}, use_global_device_ids=true | all-gather | bytes 122880 | tf_op jit(solution)/shard_map/all_gather | solution.py:27
  48.6 2.6 %fusion.7 = f32[32,1280]{1,0:T(8,128)S(1)} fusion(bf16[1,1280,1280]{2,1,0:T(8,128)(2,1)} %param.7, bf16[1,32,1280]{2,1,0:T(8,128)(2,1)S(1)} %all_gather.7), kind=kOutput, calls=%fused_computation.8 | convolution fusion | flops 104857600 | bytes 3522560 | tf_op jit(solution)/shard_map/dot_general | solution.py:35
  52.6 2.1 %fusion.32 = bf16[32,1280]{1,0:T(8,128)(2,1)S(1)} fusion(f32[32,1280]{1,0:T(8,128)S(1)} %fusion.7, bf16[1,1280,1280]{2,1,0:T(8,128)(2,1)S(1)} %copy-done, bf16[1,32,1280]{2,1,0:T(8,128)(2,1)} %all_gather.6), kind=kOutput, calls=%fused_computation.41 | convolution fusion | flops 105676800 | bytes 3604480 | tf_op jit(solution)/shard_map/bd,fd->bf/dot_general | solution.py:44
  55.3 1.7 fusion.5
  57.1 3.6 %fusion.4 = bf16[1,1280,1280]{2,1,0:T(8,128)(2,1)} fusion(bf16[32,1280]{1,0:T(8,128)(2,1)} %copy-done.2, bf16[1,32,1280]{2,1,0:T(8,128)(2,1)S(1)} %all_gather.7), kind=kOutput, calls=%fused_computation.5 | convolution fusion | flops 106496000 | bytes 3440640 | tf_op jit(solution)/shard_map/bd,bf->df/dot_general | solution.py:46
  64.8 5.6 %all-to-all-start.3 = ((bf16[16,2,640]{2,1,0:T(2,128)(2,1)}), bf16[16,2,640]{2,1,0:T(2,128)(2,1)S(1)}, u32[]{:S(2)}, u32[]{:S(2)}) async-start(bf16[16,2,640]{2,1,0:T(2,128)(2,1)} %reshape.42), calls=%async_computation.5 | async-start | bytes 81920 | tf_op jit(solution)/shard_map/all_to_all | solution.py:41
  70.4 4.8 %reduce-scatter.3.cloned.1.call-done = f32[32,640]{1,0:T(8,128)} async-done(((f32[32,1280]{1,0:T(8,128)}), f32[32,640]{1,0:T(8,128)}) %reduce-scatter.3.cloned.1.call-update) | async-done | bytes 81936 | tf_op jit(solution)/shard_map/reduce_scatter | solution.py:50
  77.7 5.6 %all-to-all-start.2 = ((bf16[16,2,640]{2,1,0:T(2,128)(2,1)}), bf16[16,2,640]{2,1,0:T(2,128)(2,1)S(1)}, u32[]{:S(2)}, u32[]{:S(2)}) async-start(bf16[16,2,640]{2,1,0:T(2,128)(2,1)} %reshape.40), calls=%async_computation.3 | async-start | bytes 81920 | tf_op jit(solution)/shard_map/all_to_all | solution.py:51
  83.7 2.0 %convolution_bitcast_fusion.2 = f32[2,256,16]{1,2,0:T(8,128)} fusion(bf16[2,256,640]{2,1,0:T(8,128)(2,1)} %param.9, bf16[16,2,640]{2,1,0:T(2,128)(2,1)S(1)} %all_to_all.43), kind=kOutput, calls=%fused_computation.31 | convolution fusion | flops 10485760 | bytes 729088 | tf_op jit(solution)/shard_map/bmd,ebd->bme/dot_general | solution.py:54
  85.7 4.4 %all-to-all-done.2 = bf16[16,2,640]{2,1,0:T(2,128)(2,1)S(1)} async-done(((bf16[16,2,640]{2,1,0:T(2,128)(2,1)}), bf16[16,2,640]{2,1,0:T(2,128)(2,1)S(1)}, u32[]{:S(2)}, u32[]{:S(2)}) %all-to-all-start.2) | async-done | bytes 40992 | tf_op jit(solution)/shard_map/all_to_all | solution.py:51
  90.3 2.0 %convolution_bitcast_fusion.1 = f32[2,256,16]{1,2,0:T(8,128)} fusion(bf16[2,256,640]{2,1,0:T(8,128)(2,1)} %param.5, bf16[16,2,640]{2,1,0:T(2,128)(2,1)S(1)} %all_to_all.41), kind=kOutput, calls=%fused_computation.30 | convolution fusion | flops 10485760 | bytes 729088 | tf_op jit(solution)/shard_map/bmd,ebd->bme/dot_general | solution.py:58
  92.4 2.3 %fusion.48 = f32[2,256,640]{2,1,0:T(8,128)} fusion(bf16[16,2,640]{2,1,0:T(2,128)(2,1)S(1)} %all_to_all.41, f32[2,16]{1,0:T(2,128)} %copy-done.7, f32[2,256,16]{1,2,0:T(8,128)S(1)} %psum.28), kind=kOutput, calls=%fused_computation.57 | convolution fusion | flops 10510623 | bytes 1384576 | tf_op jit(solution)/shard_map/bme,ebd->bmd/dot_general | solution.py:67
  94.6 15.1 %all-reduce.3.cloned.1.call-done = (f32[2,256,16]{1,2,0:T(8,128)}, f32[2,256,16]{1,2,0:T(8,128)}) async-done(((f32[2,256,16]{1,2,0:T(8,128)}, f32[2,256,16]{1,2,0:T(8,128)}), (f32[2,256,16]{1,2,0:T(8,128)}, f32[2,256,16]{1,2,0:T(8,128)})) %all-reduce.3.cloned.1.call-update) | async-done | bytes 65552 | tf_op jit(solution)/shard_map/psum | solution.py:61
  110.7 1.3 convolution_bitcast_fusion
  112.0 61.4 %psum.31 = f32[640,16]{0,1:T(8,128)} all-reduce(f32[640,16]{0,1:T(8,128)S(1)} %convolution_bitcast_fusion), channel_id=1, replica_groups=mesh['ep'=16,'tp'=2] {'ep'}, use_global_device_ids=true, to_apply=%region_11.0 | all-reduce | flops 10240 | bytes 81920 | tf_op jit(solution)/shard_map/psum | solution.py:74
  173.4 2.6 %fusion.13 = bf16[2,256,640]{2,1,0:T(8,128)(2,1)} fusion(f32[2,256,640]{2,1,0:T(8,128)} %fusion.48, f32[2,256,16]{1,2,0:T(8,128)S(1)} %fusion.24, f32[2,256,16]{1,2,0:T(8,128)} %get-tuple-element.4, bf16[640,16]{0,1:T(8,128)(2,1)S(1)} %copy-done.4, f32[2,256,16]{1,2,0:T(8,128)S(1)} %copy-done.3, f32[2,256]{1,0:T(2,128)S(1)} %copy-done.6), kind=kOutput, calls=%fused_computation.15 | convolution fusion | flops 11198991 | bytes 2086912 | tf_op jit(solution)/shard_map/bme,de->bmd/dot_general | solution.py:70
  (50 shorter events, 14.1 us)
Async XLA Ops:
  7.2 44.0 %copy-start = (bf16[1,1280,1280]{2,1,0:T(8,128)(2,1)S(1)}, bf16[1,1280,1280]{2,1,0:T(8,128)(2,1)}, u32[]{:S(2)}) copy-start(bf16[1,1280,1280]{2,1,0:T(8,128)(2,1)} %param.8) | copy-start | bytes 9830404
  19.2 1.9 %copy-start.5 = (f32[2,256]{1,0:T(2,128)}, f32[2,256]{1,0:T(2,128)S(1)}, u32[]{:S(2)}) copy-start(f32[2,256]{1,0:T(2,128)S(1)} %get-tuple-element.7) | copy-start | bytes 6148
  21.2 12.5 %all-to-all-start = ((bf16[16,2,640]{2,1,0:T(2,128)(2,1)}), bf16[16,2,640]{2,1,0:T(2,128)(2,1)S(1)}, u32[]{:S(2)}, u32[]{:S(2)}) async-start(bf16[16,2,640]{2,1,0:T(2,128)(2,1)} %copy.20), calls=%async_computation | async-start | bytes 81920 | tf_op jit(solution)/shard_map/all_to_all | solution.py:24
  27.7 9.5 %copy-start.7 = (f32[2,16]{1,0:T(2,128)}, f32[2,16]{1,0:T(2,128)S(1)}, u32[]{:S(2)}) copy-start(f32[2,16]{1,0:T(2,128)S(1)} %get-tuple-element.5) | copy-start | bytes 388
  33.7 10.2 %all-to-all-start.1 = ((bf16[16,2,640]{2,1,0:T(2,128)(2,1)}), bf16[16,2,640]{2,1,0:T(2,128)(2,1)S(1)}, u32[]{:S(2)}, u32[]{:S(2)}) async-start(bf16[16,2,640]{2,1,0:T(2,128)(2,1)} %copy.21), calls=%async_computation.1 | async-start | bytes 81920 | tf_op jit(solution)/shard_map/all_to_all | solution.py:23
  37.2 24.6 %reduce-scatter.5.cloned.1.call-start = ((), (), s32[]{:S(2)}) async-start(), calls=%async_computation.7 | async-start | bytes 245760 | tf_op jit(solution)/shard_map/reduce_scatter | solution.py:38
  52.5 22.8 %reduce-scatter.3.cloned.1.call-start = ((), (), s32[]{:S(2)}) async-start(), calls=%async_computation.6 | async-start | bytes 245760 | tf_op jit(solution)/shard_map/reduce_scatter | solution.py:50
  52.5 2.8 %copy-start.1 = (bf16[1,1280,1280]{2,1,0:T(8,128)(2,1)S(1)}, bf16[1,1280,1280]{2,1,0:T(8,128)(2,1)}, u32[]{:S(2)}) copy-start(bf16[1,1280,1280]{2,1,0:T(8,128)(2,1)} %param.7) | copy-start | bytes 9830404
  54.7 0.6 copy-start.2
  60.8 48.9 %copy-start.8 = (f32[2,16]{1,0:T(2,128)S(1)}, f32[2,16]{1,0:T(2,128)}, u32[]{:S(2)}) copy-start(f32[2,16]{1,0:T(2,128)} %copy-done.7) | copy-start | bytes 388
  60.8 49.9 %copy-start.3 = (f32[2,256,16]{1,2,0:T(8,128)S(1)}, f32[2,256,16]{1,2,0:T(8,128)}, u32[]{:S(2)}) copy-start(f32[2,256,16]{1,2,0:T(8,128)} %get-tuple-element.8) | copy-start | bytes 98308
  60.8 49.9 %copy-start.6 = (f32[2,256]{1,0:T(2,128)S(1)}, f32[2,256]{1,0:T(2,128)}, u32[]{:S(2)}) copy-start(f32[2,256]{1,0:T(2,128)} %copy-done.5) | copy-start | bytes 6148
  60.8 112.7 %copy-start.4 = (bf16[640,16]{0,1:T(8,128)(2,1)S(1)}, bf16[640,16]{0,1:T(8,128)(2,1)}, u32[]{:S(2)}) copy-start(bf16[640,16]{0,1:T(8,128)(2,1)} %param.6) | copy-start | bytes 61444
  64.8 12.9 %all-to-all-start.3 = ((bf16[16,2,640]{2,1,0:T(2,128)(2,1)}), bf16[16,2,640]{2,1,0:T(2,128)(2,1)S(1)}, u32[]{:S(2)}, u32[]{:S(2)}) async-start(bf16[16,2,640]{2,1,0:T(2,128)(2,1)} %reshape.42), calls=%async_computation.5 | async-start | bytes 81920 | tf_op jit(solution)/shard_map/all_to_all | solution.py:41
  77.7 12.3 %all-to-all-start.2 = ((bf16[16,2,640]{2,1,0:T(2,128)(2,1)}), bf16[16,2,640]{2,1,0:T(2,128)(2,1)S(1)}, u32[]{:S(2)}, u32[]{:S(2)}) async-start(bf16[16,2,640]{2,1,0:T(2,128)(2,1)} %reshape.40), calls=%async_computation.3 | async-start | bytes 81920 | tf_op jit(solution)/shard_map/all_to_all | solution.py:51
  83.4 26.3 %all-reduce.3.cloned.1.call-start = ((), (), s32[]{:S(2)}) async-start(), calls=%async_computation.8 | async-start | bytes 131072 | tf_op jit(solution)/shard_map/psum | solution.py:61
Sparse Core Ops, SparseCore 0:
  52.6 9.1 reduce-scatter.4
  64.6 10.5 reduce-scatter.2
  92.5 17.1 all-reduce.2
where the time goes:
time: 183 us
  blocking collectives  80.8 us (44%)
  waiting for transfers between devices  31.2 us (17%)
  matrix products  25.7 us (14%)
  starting transfers between devices  20.7 us (11%)
  between operations  13.9 us (8%)
  other arithmetic  5.82 us (3%)
  local copies, waits for them, and re-layouts  4.5 us (2%)
    psum x1, blocking collectives, on_device(): grad_router = lax.psum(router_part, 'ep')  61.4 us
    psum x1, waiting for transfers between devices, on_device(): dispatch_dot = lax.psum(dispatch_part, 'tp')  15.1 us
    psum x1, blocking collectives, on_device(): logits = lax.psum(partial_logits, 'tp')  9.93 us
    all_to_all x1, starting transfers between devices, on_device(): lax.all_to_all(grad_half, 'ep', split_axis=0, concat_axis=1, tiled=True)  5.81 us
    all_to_all x1, starting transfers between devices, on_device(): lax.all_to_all(in_share.reshape(1, all_rows, -1), 'ep', split_axis=1, con...  5.61 us
    all_to_all x1, starting transfers between devices, on_device(): lax.all_to_all(out_share.reshape(1, all_rows, -1), 'ep', split_axis=1, co...  5.61 us
    reduce_scatter x1, waiting for transfers between devices, on_device(): lax.psum_scatter(in_part, 'tp', scatter_dimension=1, tiled=True)  4.83 us
    all_gather x1, blocking collectives, on_device(): lax.all_gather(sent_grad, 'tp', axis=2, tiled=True)  4.79 us
  transfers between devices with their start and end apart: 7, of which 6 were waited for; matrix products, arithmetic and copies ran while one was open for 11% of the time, Pallas kernels for 0%

commit v1 on v0

v1 whole, which is shorter than its diff:
```python
import functools

import jax
import jax.numpy as jnp
from jax import lax
from jax.experimental import pallas as pl
from jax.experimental.pallas import tpu as pltpu
from jax.sharding import PartitionSpec as P

F32 = jnp.float32
BF16 = jnp.bfloat16
MESH = pl.DeviceIdType.MESH

LOGITS, SLOTS, OUT, IN, LOGIT_GRAD, SCATTER, GATHER = range(7)


def nt(a, b):
    return lax.dot_general(a, b, (((1,), (1,)), ((), ())), preferred_element_type=F32)


def tn(a, b):
    return lax.dot_general(a, b, (((0,), (0,)), ((), ())), preferred_element_type=F32)


def nn(a, b):
    return jnp.dot(a, b, preferred_element_type=F32)


def gelu_parts(v):
    c = 0.7978845608028654
    t = jnp.tanh(c * (v + 0.044715 * (v * v * v)))
    half = 0.5 * (1.0 + t)
    slope = half + (0.5 * c) * v * (1.0 - t * t) * (1.0 + (3.0 * 0.044715) * (v * v))
    return v * half, slope


def kernel(
    n_ep,
    tok_h, router_h, w_in_h, w_out_h, grad_h,
    grad_tokens_o, grad_router_o, grad_w_o,
    tok, router, w_in, w_out, grad,
    logits_s, logits_r, slots_s, slots_r, slot_in, slot_grad, pre_grad,
    out_s, out_r, in_s, in_r, lg_s, lg_r, rs_s, rs_r, ag,
    load_sem, send_sem, recv_sem,
):
    ep, tp = lax.axis_index("ep"), lax.axis_index("tp")
    other = 1 - tp
    n_all = 2 * n_ep
    me = tp * n_ep + ep
    images, patches, width = tok.shape
    experts = router.shape[0]
    rows = n_ep * images

    loads = [
        pltpu.make_async_copy(src, dst, load_sem.at[i])
        for i, (src, dst) in enumerate(
            ((tok_h, tok), (router_h, router), (grad_h, grad), (w_in_h, w_in), (w_out_h, w_out))
        )
    ]
    for load in loads:
        load.start()

    barrier = pltpu.get_barrier_semaphore()

    def greet(off, carry):
        q = lax.rem(me + off, n_all)
        pl.semaphore_signal(
            barrier, inc=1, device_id=(lax.rem(q, n_ep), q // n_ep), device_id_type=MESH
        )
        return carry

    lax.fori_loop(1, n_all, greet, 0)

    def to_partner(src, dst, k):
        return pltpu.make_async_remote_copy(
            src_ref=src, dst_ref=dst, send_sem=send_sem.at[k], recv_sem=recv_sem.at[k],
            device_id=(ep, other), device_id_type=MESH,
        )

    def send_all(src, by_expert, dst, k):
        def step(off, carry):
            q = lax.rem(me + off, n_all)
            to_ep, to_tp = lax.rem(q, n_ep), q // n_ep
            pltpu.make_async_remote_copy(
                src_ref=src.at[to_ep if by_expert else q], dst_ref=dst.at[me],
                send_sem=send_sem.at[k], recv_sem=recv_sem.at[k],
                device_id=(to_ep, to_tp), device_id_type=MESH,
            ).start()
            return carry

        lax.fori_loop(1, n_all, step, 0)

    def send_row(src, dst, k):
        def step(off, carry):
            to_ep = lax.rem(ep + off, n_ep)
            pltpu.make_async_remote_copy(
                src_ref=src(to_ep), dst_ref=dst.at[ep],
                send_sem=send_sem.at[k], recv_sem=recv_sem.at[k],
                device_id=(to_ep, tp), device_id_type=MESH,
            ).start()
            return carry

        lax.fori_loop(1, n_ep, step, 0)

    def wait_blocks(ref, count, sem):
        blocks = ref.at[pl.ds(0, count)]
        pltpu.make_async_copy(blocks, blocks, sem).wait()

    loads[0].wait()
    loads[1].wait()
    router_t = router[...]
    tok_rows = tok[...].reshape(images * patches, width)
    logits_s[...] = nt(router_t, tok_rows)
    pl.semaphore_wait(barrier, n_all - 1)
    swap = to_partner(logits_s, logits_r, LOGITS)
    swap.start()
    swap.wait()
    logits = logits_s[...] + logits_r[...]

    def per_image(x):
        return [x[:, b * patches : (b + 1) * patches] for b in range(images)]

    def softmax(x, axis):
        e = jnp.exp(x - jnp.max(x, axis=axis, keepdims=True))
        return e / jnp.sum(e, axis=axis, keepdims=True)

    dispatch = [softmax(x, 1) for x in per_image(logits)]
    combine = [softmax(x, 0) for x in per_image(logits)]
    dispatch_b = [x.astype(BF16) for x in dispatch]

    loads[2].wait()
    halves = [nn(dispatch_b[b], tok[b]) for b in range(images)]
    halves += [nn(combine[b].astype(BF16), grad[b]) for b in range(images)]
    slots_s[...] = jnp.stack(halves, axis=1).astype(BF16)
    slots_r[me] = slots_s[ep]
    send_all(slots_s, True, slots_r, SLOTS)

    loads[3].wait()
    loads[4].wait()
    wait_blocks(slots_r, n_all - 1, recv_sem.at[SLOTS])
    for s in range(2):
        half = slots_r[s * n_ep : (s + 1) * n_ep].astype(F32)
        cols = slice(s * width, (s + 1) * width)
        slot_in[:, cols] = half[:, :images].reshape(rows, width).astype(BF16)
        slot_grad[:, cols] = half[:, images:].reshape(rows, width).astype(BF16)

    def pieces(part, ref):
        for s in range(2):
            cut = part[:, s * width : (s + 1) * width]
            ref[s * n_ep : (s + 1) * n_ep] = cut.reshape(n_ep, images, width).astype(BF16)

    pre = nn(slot_in[...], w_in[...])
    act, slope = gelu_parts(pre)
    pieces(nn(act.astype(BF16), w_out[...]), out_s)
    out_r[me] = out_s[me]
    send_all(out_s, False, out_r, OUT)
    pre_grad[...] = (slope * nt(slot_grad[...], w_out[...])).astype(BF16)
    pieces(nt(pre_grad[...], w_in[...]), in_s)
    in_r[me] = in_s[me]
    send_all(in_s, False, in_r, IN)

    tile = 256 if grad_w_o.shape[0] % 256 == 0 else 128

    def grad_w_tile(i, carry):
        at = pl.ds(pl.multiple_of(i * tile, tile), tile)
        grad_w_o[at, :] = tn(slot_in[:, at], pre_grad[...]).astype(BF16)
        return carry

    lax.fori_loop(0, grad_w_o.shape[0] // tile, grad_w_tile, 0)

    def both_halves(ref):
        total = ref[:n_ep].astype(F32) + ref[n_ep:].astype(F32)
        return [total[:, b, :].astype(BF16) for b in range(images)]

    wait_blocks(out_r, n_all - 1, recv_sem.at[OUT])
    slot_out = both_halves(out_r)
    shares = []
    for b in range(images):
        dot = nt(slot_out[b], grad[b])
        shares.append(combine[b] * (dot - jnp.sum(combine[b] * dot, axis=0, keepdims=True)))
    wait_blocks(in_r, n_all - 1, recv_sem.at[IN])
    slot_in_grad = both_halves(in_r)
    for b in range(images):
        dot = nt(slot_in_grad[b], tok[b])
        shares[b] += dispatch[b] * (dot - jnp.sum(dispatch[b] * dot, axis=1, keepdims=True))
        lg_s[:, b * patches : (b + 1) * patches] = shares[b]
    swap_lg = to_partner(lg_s, lg_r, LOGIT_GRAD)
    swap_lg.start()
    swap_lg.wait()
    logit_b = (lg_s[...] + lg_r[...]).astype(BF16)

    part = nn(logit_b, tok_rows)
    rs_s[...] = part.reshape(n_ep, experts // n_ep, width)
    rs_r[ep] = rs_s[ep]
    send_row(lambda to_ep: rs_s.at[to_ep], rs_r, SCATTER)

    def tokens_of(b):
        left = jnp.concatenate([dispatch_b[b], per_image(logit_b)[b]], axis=0)
        right = jnp.concatenate([slot_in_grad[b], router_t], axis=0)
        grad_tokens_o[b] = tn(left, right).astype(BF16)

    for b in range(images // 2):
        tokens_of(b)
    wait_blocks(rs_r, n_ep - 1, recv_sem.at[SCATTER])
    ag[ep] = jnp.sum(rs_r[...], axis=0)
    send_row(lambda to_ep: ag.at[ep], ag, GATHER)
    for b in range(images // 2, images):
        tokens_of(b)
    wait_blocks(ag, n_ep - 1, recv_sem.at[GATHER])
    grad_router_o[...] = ag[...].reshape(experts, width)

    wait_blocks(slots_r, n_all - 1, send_sem.at[SLOTS])
    wait_blocks(out_r, n_all - 1, send_sem.at[OUT])
    wait_blocks(in_r, n_all - 1, send_sem.at[IN])
    wait_blocks(rs_r, n_ep - 1, send_sem.at[SCATTER])
    wait_blocks(ag, n_ep - 1, send_sem.at[GATHER])


def on_device(n_ep, tokens, router, w_in, w_out, grad_out):
    images, patches, width = tokens.shape
    experts = router.shape[1]
    w_in, w_out = w_in[0], w_out[0]
    model, hidden = w_in.shape
    rows = n_ep * images
    n_all = 2 * n_ep
    vmem = pltpu.VMEM
    grad_tokens, grad_router, grad_w = pl.pallas_call(
        functools.partial(kernel, n_ep),
        out_shape=(
            OUT_SPACE(tokens.shape, BF16),
            OUT_SPACE((experts, width), F32),
            OUT_SPACE(w_in.shape, BF16),
        ),
        in_specs=[pl.BlockSpec(memory_space=pltpu.HBM)] * 5,
        out_specs=(pl.BlockSpec(memory_space=pltpu.VMEM),) * 3,
        scratch_shapes=[
            vmem(tokens.shape, BF16),
            vmem((experts, width), BF16),
            vmem(w_in.shape, BF16),
            vmem(w_out.shape, BF16),
            vmem(grad_out.shape, BF16),
            vmem((experts, images * patches), F32),
            vmem((experts, images * patches), F32),
            vmem((experts, 2 * images, width), BF16),
            vmem((n_all, 2 * images, width), BF16),
            vmem((rows, model), BF16),
            vmem((rows, model), BF16),
            vmem((rows, hidden), BF16),
            vmem((n_all, images, width), BF16),
            vmem((n_all, images, width), BF16),
            vmem((n_all, images, width), BF16),
            vmem((n_all, images, width), BF16),
            vmem((experts, images * patches), F32),
            vmem((experts, images * patches), F32),
            vmem((n_ep, experts // n_ep, width), F32),
            vmem((n_ep, experts // n_ep, width), F32),
            vmem((n_ep, experts // n_ep, width), F32),
            pltpu.SemaphoreType.DMA((5,)),
            pltpu.SemaphoreType.DMA((7,)),
            pltpu.SemaphoreType.DMA((7,)),
        ],
        compiler_params=pltpu.CompilerParams(
            collective_id=0, has_side_effects=True, vmem_limit_bytes=40 * 1024 * 1024
        ),
    )(*(pltpu.with_memory_space_constraint(x, pltpu.HBM) for x in (tokens, router.T, w_in, w_out, grad_out)))
    return grad_tokens, grad_router.T, grad_w.reshape(1, model, hidden)


OUT_SPACE = pltpu.VMEM


def solution(mesh):
    placed = (
        P("ep", None, "tp"),
        P("tp", None),
        P("ep", None, "tp"),
        P("ep", "tp", None),
        P("ep", None, "tp"),
    )
    return jax.shard_map(
        functools.partial(on_device, mesh.shape["ep"]),
        mesh=mesh,
        in_specs=placed,
        out_specs=(P("ep", None, "tp"), P("tp", None), P("ep", None, "tp")),
        check_vma=False,
    )
```

time: 183 us -> 40.4 us (0.22)
  blocking collectives: 80.8 us -> 0 us
  Pallas kernels: 0 us -> 36.5 us
  waiting for transfers between devices: 31.2 us -> 0 us
  matrix products: 25.7 us -> 0 us
  starting transfers between devices: 20.7 us -> 0 us
  between operations: 13.9 us -> 0.64 us
  other arithmetic: 5.82 us -> 0 us
    psum x2 -> x0, blocking collectives: 71.3 us -> none  [the longest x1 61.4 us: on_device(): grad_router = lax.psum(router_part, 'ep')]
    pallas_call x0 -> x1, Pallas kernels: none -> 36.5 us  [on_device(): pl.pallas_call(functools.partial(kernel, n_ep), out_shape=(OUT_SPACE(toke...]
    dot_general x13 -> x0, matrix products: 25.7 us -> none  [the longest x1 3.65 us: on_device(): jnp.einsum('bd,bf->df', slot_in, pre_grad, preferred_element_type=jnp.flo...]
    all_to_all x4 -> x0, starting transfers between devices: 20.5 us -> none  [the longest x1 5.81 us: on_device(): lax.all_to_all(grad_half, 'ep', split_axis=0, concat_axis=1, tiled=True)]
    psum x1 -> x0, waiting for transfers between devices: 15.1 us -> none  [on_device(): dispatch_dot = lax.psum(dispatch_part, 'tp')]
    all_to_all x4 -> x0, waiting for transfers between devices: 10.2 us -> none  [the longest x1 4.37 us: on_device(): lax.all_to_all(in_share.reshape(1, all_rows, -1), 'ep', split_axis=1, con...]
    all_gather x2 -> x0, blocking collectives: 9.46 us -> none  [the longest x1 4.79 us: on_device(): lax.all_gather(sent_grad, 'tp', axis=2, tiled=True)]
    reduce_scatter x2 -> x0, waiting for transfers between devices: 5.9 us -> none  [the longest x1 4.83 us: on_device(): lax.psum_scatter(in_part, 'tp', scatter_dimension=1, tiled=True)]
  transfers between devices with their start and end apart: 7 -> 0, of which waited for: 6 -> 0; matrix products, arithmetic and copies ran while one was open for 11% -> 0% of each run, Pallas kernels for 0% -> 0%
where the time goes in v1:
time: 40.4 us; the launch traced here: 40.3 us
  Pallas kernels  36.5 us (90%)
  local copies, waits for them, and re-layouts  3.16 us (8%)
  between operations  0.64 us (2%)
    pallas_call x1, Pallas kernels, on_device(): pl.pallas_call(functools.partial(kernel, n_ep), out_shape=(OUT_SPACE(toke...  36.5 us
    unnamed x3, local copies, waits for them, and re-layouts  3.16 us

profile of v1, /device:TPU:0, one launch (start us, length us, event | category | flops | bytes accessed | tf_op | source)
XLA Modules:
  0.0 40.3 jit_solution(4368763032888864545)
XLA Ops:
  0.6 36.5 %shard_map.76 = (bf16[2,256,640]{2,1,0:T(8,128)(2,1)S(1)}, f32[16,640]{1,0:T(8,128)S(1)}, bf16[1280,1280]{1,0:T(8,128)(2,1)S(1)}) custom-call(bf16[2,256,640]{2,1,0:T(8,128)(2,1)} %tok_h.1, bf16[16,640]{1,0:T(8,128)(2,1)} %bitcast.9, bf16[1280,1280]{1,0:T(8,128)(2,1)} %bitcast.7, bf16[1280,1280]{1,0:T(8,128)(2,1)} %bitcast.8, bf16[2,256,640]{2,1,0:T(8,128)(2,1)} %grad_h.1), custom_call_target="tpu_custom_call" | custom-call | tf_op jit(solution)/shard_map/pallas_call | solution.py:227
  37.1 0.8 %copy.11 = bf16[2,256,640]{2,1,0:T(8,128)(2,1)} copy(bf16[2,256,640]{2,1,0:T(8,128)(2,1)S(1)} %get-tuple-element.9) | data formatting | bytes 1310720
  37.9 0.6 %copy.12 = f32[640,16]{0,1:T(8,128)} copy(f32[640,16]{0,1:T(8,128)S(1)} %bitcast.6) | data formatting | bytes 81920
  38.6 1.7 %copy.13 = bf16[1,1280,1280]{2,1,0:T(8,128)(2,1)} copy(bf16[1,1280,1280]{2,1,0:T(8,128)(2,1)S(1)} %bitcast.5) | data formatting | bytes 6553600

commit v2 on v1

--- a/solution.py
+++ b/solution.py
@@ -62,14 +62,25 @@
 
     barrier = pltpu.get_barrier_semaphore()
 
-    def greet(off, carry):
-        q = lax.rem(me + off, n_all)
-        pl.semaphore_signal(
-            barrier, inc=1, device_id=(lax.rem(q, n_ep), q // n_ep), device_id_type=MESH
-        )
-        return carry
-
-    lax.fori_loop(1, n_all, greet, 0)
+    def wrapped(off):
+        to = ep + off
+        return jnp.where(to >= n_ep, to - n_ep, to)
+
+    def others(act):
+        group = next(k for k in (5, 3, 1) if (n_ep - 1) % k == 0)
+
+        def step(i, carry):
+            for j in range(group):
+                act(wrapped(i * group + (j + 1)))
+            return carry
+
+        lax.fori_loop(0, (n_ep - 1) // group, step, 0)
+
+    def greet(to_ep, to_tp):
+        pl.semaphore_signal(barrier, inc=1, device_id=(to_ep, to_tp), device_id_type=MESH)
+
+    greet(ep, other)
+    others(lambda to_ep: (greet(to_ep, tp), greet(to_ep, other)))
 
     def to_partner(src, dst, k):
         return pltpu.make_async_remote_copy(
@@ -78,29 +89,25 @@
         )
 
     def send_all(src, by_expert, dst, k):
-        def step(off, carry):
-            q = lax.rem(me + off, n_all)
-            to_ep, to_tp = lax.rem(q, n_ep), q // n_ep
+        def send(to_ep, to_tp):
             pltpu.make_async_remote_copy(
-                src_ref=src.at[to_ep if by_expert else q], dst_ref=dst.at[me],
+                src_ref=src.at[to_ep if by_expert else to_tp * n_ep + to_ep], dst_ref=dst.at[me],
                 send_sem=send_sem.at[k], recv_sem=recv_sem.at[k],
                 device_id=(to_ep, to_tp), device_id_type=MESH,
             ).start()
-            return carry
-
-        lax.fori_loop(1, n_all, step, 0)
+
+        others(lambda to_ep: (send(to_ep, tp), send(to_ep, other)))
+        send(ep, other)
 
     def send_row(src, dst, k):
-        def step(off, carry):
-            to_ep = lax.rem(ep + off, n_ep)
+        def send(to_ep):
             pltpu.make_async_remote_copy(
                 src_ref=src(to_ep), dst_ref=dst.at[ep],
                 send_sem=send_sem.at[k], recv_sem=recv_sem.at[k],
                 device_id=(to_ep, tp), device_id_type=MESH,
             ).start()
-            return carry
-
-        lax.fori_loop(1, n_ep, step, 0)
+
+        others(send)
 
     def wait_blocks(ref, count, sem):
         blocks = ref.at[pl.ds(0, count)]
@@ -216,6 +223,17 @@
     wait_blocks(ag, n_ep - 1, send_sem.at[GATHER])
 
 
+def write_out(tokens_v, router_v, w_v, tokens_o, router_o, w_o, sem):
+    cut = w_v.shape[0] // 4
+    pairs = [(w_v.at[pl.ds(i * cut, cut)], w_o.at[pl.ds(i * cut, cut)]) for i in range(4)]
+    pairs += [(tokens_v, tokens_o), (router_v, router_o)]
+    copies = [pltpu.make_async_copy(a, b, sem.at[i]) for i, (a, b) in enumerate(pairs)]
+    for copy in copies:
+        copy.start()
+    for copy in copies:
+        copy.wait()
+
+
 def on_device(n_ep, tokens, router, w_in, w_out, grad_out):
     images, patches, width = tokens.shape
     experts = router.shape[1]
@@ -227,9 +245,9 @@
     grad_tokens, grad_router, grad_w = pl.pallas_call(
         functools.partial(kernel, n_ep),
         out_shape=(
-            OUT_SPACE(tokens.shape, BF16),
-            OUT_SPACE((experts, width), F32),
-            OUT_SPACE(w_in.shape, BF16),
+            pltpu.VMEM(tokens.shape, BF16),
+            pltpu.VMEM((experts, width), F32),
+            pltpu.VMEM(w_in.shape, BF16),
         ),
         in_specs=[pl.BlockSpec(memory_space=pltpu.HBM)] * 5,
         out_specs=(pl.BlockSpec(memory_space=pltpu.VMEM),) * 3,
@@ -263,10 +281,15 @@
             collective_id=0, has_side_effects=True, vmem_limit_bytes=40 * 1024 * 1024
         ),
     )(*(pltpu.with_memory_space_constraint(x, pltpu.HBM) for x in (tokens, router.T, w_in, w_out, grad_out)))
+    results = (grad_tokens, grad_router, grad_w)
+    grad_tokens, grad_router, grad_w = pl.pallas_call(
+        write_out,
+        out_shape=tuple(jax.ShapeDtypeStruct(x.shape, x.dtype) for x in results),
+        in_specs=[pl.BlockSpec(memory_space=pltpu.VMEM)] * 3,
+        out_specs=(pl.BlockSpec(memory_space=pltpu.HBM),) * 3,
+        scratch_shapes=[pltpu.SemaphoreType.DMA((6,))],
+    )(*results)
     return grad_tokens, grad_router.T, grad_w.reshape(1, model, hidden)
-
-
-OUT_SPACE = pltpu.VMEM
 
 
 def solution(mesh):

time: 40.4 us -> 44.3 us (1.097)
  Pallas kernels: 36.5 us -> 40.4 us
    pallas_call x1 -> x2, Pallas kernels: 36.5 us -> 40.4 us  [the longest x1 36.2 us: on_device(): pl.pallas_call(functools.partial(kernel, n_ep), out_shape=(pltpu.VMEM(tok...]
    unnamed x3 -> x6, local copies, waits for them, and re-layouts: 3.16 us -> 3.1 us
where the time goes in v2:
time: 44.3 us; the launch traced here: 44.1 us
  Pallas kernels  40.4 us (91%)
  local copies, waits for them, and re-layouts  3.1 us (7%)
  between operations  0.65 us (1%)
    pallas_call x1, Pallas kernels, on_device(): pl.pallas_call(functools.partial(kernel, n_ep), out_shape=(pltpu.VMEM(tok...  36.2 us
    pallas_call x1, Pallas kernels, on_device(): pl.pallas_call(write_out, out_shape=tuple((jax.ShapeDtypeStruct(x.shape,...  4.12 us
    unnamed x6, local copies, waits for them, and re-layouts  3.1 us

profile of v2, /device:TPU:0, one launch (start us, length us, event | category | flops | bytes accessed | tf_op | source)
XLA Modules:
  0.0 44.1 jit_solution(9666518684909022279)
XLA Ops:
  0.6 36.2 %shard_map.76 = (bf16[2,256,640]{2,1,0:T(8,128)(2,1)S(1)}, f32[16,640]{1,0:T(8,128)S(1)}, bf16[1280,1280]{1,0:T(8,128)(2,1)S(1)}) custom-call(bf16[2,256,640]{2,1,0:T(8,128)(2,1)} %tok_h.1, bf16[16,640]{1,0:T(8,128)(2,1)} %bitcast.7, bf16[1280,1280]{1,0:T(8,128)(2,1)} %bitcast.5, bf16[1280,1280]{1,0:T(8,128)(2,1)} %bitcast.6, bf16[2,256,640]{2,1,0:T(8,128)(2,1)} %grad_h.1), custom_call_target="tpu_custom_call" | custom-call | tf_op jit(solution)/shard_map/pallas_call | solution.py:245
  36.9 0.0 copy-start
  36.9 1.7 %copy-done = bf16[1280,1280]{1,0:T(8,128)(2,1)} copy-done((bf16[1280,1280]{1,0:T(8,128)(2,1)}, bf16[1280,1280]{1,0:T(8,128)(2,1)S(1)}, u32[]{:S(2)}) %copy-start) | copy-done | bytes 3276824
  38.5 0.0 copy-start.1
  38.5 0.8 %copy-done.1 = bf16[2,256,640]{2,1,0:T(8,128)(2,1)} copy-done((bf16[2,256,640]{2,1,0:T(8,128)(2,1)}, bf16[2,256,640]{2,1,0:T(8,128)(2,1)S(1)}, u32[]{:S(2)}) %copy-start.1) | copy-done | bytes 655384
  39.4 0.0 copy-start.2
  39.4 0.6 %copy-done.2 = f32[16,640]{1,0:T(8,128)} copy-done((f32[16,640]{1,0:T(8,128)}, f32[16,640]{1,0:T(8,128)S(1)}, u32[]{:S(2)}) %copy-start.2) | copy-done | bytes 40984
  40.0 4.1 %shard_map.77 = (bf16[2,256,640]{2,1,0:T(8,128)(2,1)}, f32[16,640]{1,0:T(8,128)}, bf16[1280,1280]{1,0:T(8,128)(2,1)}) custom-call(bf16[2,256,640]{2,1,0:T(8,128)(2,1)} %copy-done.1, f32[16,640]{1,0:T(8,128)} %copy-done.2, bf16[1280,1280]{1,0:T(8,128)(2,1)} %copy-done), custom_call_target="tpu_custom_call" | custom-call | tf_op jit(solution)/shard_map/pallas_call | solution.py:285
Async XLA Ops:
  36.9 1.7 %copy-start = (bf16[1280,1280]{1,0:T(8,128)(2,1)}, bf16[1280,1280]{1,0:T(8,128)(2,1)S(1)}, u32[]{:S(2)}) copy-start(bf16[1280,1280]{1,0:T(8,128)(2,1)S(1)} %get-tuple-element.11.w_v) | copy-start | bytes 9830404
  38.5 0.8 %copy-start.1 = (bf16[2,256,640]{2,1,0:T(8,128)(2,1)}, bf16[2,256,640]{2,1,0:T(8,128)(2,1)S(1)}, u32[]{:S(2)}) copy-start(bf16[2,256,640]{2,1,0:T(8,128)(2,1)S(1)} %get-tuple-element.9.tokens_v) | copy-start | bytes 1966084
  39.4 0.6 %copy-start.2 = (f32[16,640]{1,0:T(8,128)}, f32[16,640]{1,0:T(8,128)S(1)}, u32[]{:S(2)}) copy-start(f32[16,640]{1,0:T(8,128)S(1)} %get-tuple-element.10.router_v) | copy-start | bytes 122884

commit v3 on v2

--- a/solution.py
+++ b/solution.py
@@ -11,7 +11,7 @@
 BF16 = jnp.bfloat16
 MESH = pl.DeviceIdType.MESH
 
-LOGITS, SLOTS, OUT, IN, LOGIT_GRAD, SCATTER, GATHER = range(7)
+LOGITS, SLOTS, GRADS, OUT, IN, LOGIT_GRAD, SCATTER, GATHER = range(8)
 
 
 def nt(a, b):
@@ -39,7 +39,7 @@
     tok_h, router_h, w_in_h, w_out_h, grad_h,
     grad_tokens_o, grad_router_o, grad_w_o,
     tok, router, w_in, w_out, grad,
-    logits_s, logits_r, slots_s, slots_r, slot_in, slot_grad, pre_grad,
+    logits_s, logits_r, slots_s, slots_r, grads_s, grads_r, slot_in, slot_grad, pre_grad,
     out_s, out_r, in_s, in_r, lg_s, lg_r, rs_s, rs_r, ag,
     load_sem, send_sem, recv_sem,
 ):
@@ -135,21 +135,25 @@
     combine = [softmax(x, 0) for x in per_image(logits)]
     dispatch_b = [x.astype(BF16) for x in dispatch]
 
+    def halves(weights, rows_of, ref_s, ref_r, k):
+        parts = [nn(weights[b], rows_of[b]) for b in range(images)]
+        ref_s[...] = jnp.stack(parts, axis=1).astype(BF16)
+        ref_r[me] = ref_s[ep]
+        send_all(ref_s, True, ref_r, k)
+
+    halves(dispatch_b, tok, slots_s, slots_r, SLOTS)
     loads[2].wait()
-    halves = [nn(dispatch_b[b], tok[b]) for b in range(images)]
-    halves += [nn(combine[b].astype(BF16), grad[b]) for b in range(images)]
-    slots_s[...] = jnp.stack(halves, axis=1).astype(BF16)
-    slots_r[me] = slots_s[ep]
-    send_all(slots_s, True, slots_r, SLOTS)
+    halves([x.astype(BF16) for x in combine], grad, grads_s, grads_r, GRADS)
+
+    def arrived(ref, dst, k):
+        wait_blocks(ref, n_all - 1, recv_sem.at[k])
+        for s in range(2):
+            half = ref[s * n_ep : (s + 1) * n_ep].astype(F32)
+            dst[:, s * width : (s + 1) * width] = half.reshape(rows, width).astype(BF16)
 
     loads[3].wait()
     loads[4].wait()
-    wait_blocks(slots_r, n_all - 1, recv_sem.at[SLOTS])
-    for s in range(2):
-        half = slots_r[s * n_ep : (s + 1) * n_ep].astype(F32)
-        cols = slice(s * width, (s + 1) * width)
-        slot_in[:, cols] = half[:, :images].reshape(rows, width).astype(BF16)
-        slot_grad[:, cols] = half[:, images:].reshape(rows, width).astype(BF16)
+    arrived(slots_r, slot_in, SLOTS)
 
     def pieces(part, ref):
         for s in range(2):
@@ -161,6 +165,7 @@
     pieces(nn(act.astype(BF16), w_out[...]), out_s)
     out_r[me] = out_s[me]
     send_all(out_s, False, out_r, OUT)
+    arrived(grads_r, slot_grad, GRADS)
     pre_grad[...] = (slope * nt(slot_grad[...], w_out[...])).astype(BF16)
     pieces(nt(pre_grad[...], w_in[...]), in_s)
     in_r[me] = in_s[me]
@@ -217,6 +222,7 @@
     grad_router_o[...] = ag[...].reshape(experts, width)
 
     wait_blocks(slots_r, n_all - 1, send_sem.at[SLOTS])
+    wait_blocks(grads_r, n_all - 1, send_sem.at[GRADS])
     wait_blocks(out_r, n_all - 1, send_sem.at[OUT])
     wait_blocks(in_r, n_all - 1, send_sem.at[IN])
     wait_blocks(rs_r, n_ep - 1, send_sem.at[SCATTER])
@@ -259,8 +265,10 @@
             vmem(grad_out.shape, BF16),
             vmem((experts, images * patches), F32),
             vmem((experts, images * patches), F32),
-            vmem((experts, 2 * images, width), BF16),
-            vmem((n_all, 2 * images, width), BF16),
+            vmem((experts, images, width), BF16),
+            vmem((n_all, images, width), BF16),
+            vmem((experts, images, width), BF16),
+            vmem((n_all, images, width), BF16),
             vmem((rows, model), BF16),
             vmem((rows, model), BF16),
             vmem((rows, hidden), BF16),
@@ -274,8 +282,8 @@
             vmem((n_ep, experts // n_ep, width), F32),
             vmem((n_ep, experts // n_ep, width), F32),
             pltpu.SemaphoreType.DMA((5,)),
-            pltpu.SemaphoreType.DMA((7,)),
-            pltpu.SemaphoreType.DMA((7,)),
+            pltpu.SemaphoreType.DMA((8,)),
+            pltpu.SemaphoreType.DMA((8,)),
         ],
         compiler_params=pltpu.CompilerParams(
             collective_id=0, has_side_effects=True, vmem_limit_bytes=40 * 1024 * 1024
@@ -288,7 +296,8 @@
         in_specs=[pl.BlockSpec(memory_space=pltpu.VMEM)] * 3,
         out_specs=(pl.BlockSpec(memory_space=pltpu.HBM),) * 3,
         scratch_shapes=[pltpu.SemaphoreType.DMA((6,))],
-    )(*results)
+        compiler_params=pltpu.CompilerParams(vmem_limit_bytes=8 * 1024 * 1024),
+    )(*(pltpu.with_memory_space_constraint(x, pltpu.VMEM) for x in results))
     return grad_tokens, grad_router.T, grad_w.reshape(1, model, hidden)
 
 

time: 44.3 us -> 38 us (0.86)
  Pallas kernels: 40.4 us -> 37.2 us
  local copies, waits for them, and re-layouts: 3.1 us -> 0 us
    unnamed x6 -> x0, local copies, waits for them, and re-layouts: 3.1 us -> none
    pallas_call x1, Pallas kernels: 4.12 us -> 1.97 us  [on_device(): pl.pallas_call(write_out, out_shape=tuple((jax.ShapeDtypeStruct(x.shape,...]
    pallas_call x1, Pallas kernels: 36.2 us -> 35.2 us  [on_device(): pl.pallas_call(functools.partial(kernel, n_ep), out_shape=(pltpu.VMEM(tok...]
where the time goes in v3:
time: 38 us; the launch traced here: 37.8 us
  Pallas kernels  37.2 us (98%)
  between operations  0.64 us (2%)
    pallas_call x1, Pallas kernels, on_device(): pl.pallas_call(functools.partial(kernel, n_ep), out_shape=(pltpu.VMEM(tok...  35.2 us
    pallas_call x1, Pallas kernels, on_device(): pl.pallas_call(write_out, out_shape=tuple((jax.ShapeDtypeStruct(x.shape,...  1.97 us

profile of v3, /device:TPU:0, one launch (start us, length us, event | category | flops | bytes accessed | tf_op | source)
XLA Modules:
  0.0 37.8 jit_solution(6668073365179663139)
XLA Ops:
  0.6 35.2 %shard_map.76 = (bf16[2,256,640]{2,1,0:T(8,128)(2,1)S(1)}, f32[16,640]{1,0:T(8,128)S(1)}, bf16[1280,1280]{1,0:T(8,128)(2,1)S(1)}) custom-call(bf16[2,256,640]{2,1,0:T(8,128)(2,1)} %tok_h.1, bf16[16,640]{1,0:T(8,128)(2,1)} %bitcast.7, bf16[1280,1280]{1,0:T(8,128)(2,1)} %bitcast.5, bf16[1280,1280]{1,0:T(8,128)(2,1)} %bitcast.6, bf16[2,256,640]{2,1,0:T(8,128)(2,1)} %grad_h.1), custom_call_target="tpu_custom_call" | custom-call | tf_op jit(solution)/shard_map/pallas_call | solution.py:251
  35.9 2.0 %shard_map.77 = (bf16[2,256,640]{2,1,0:T(8,128)(2,1)}, f32[16,640]{1,0:T(8,128)}, bf16[1280,1280]{1,0:T(8,128)(2,1)}) custom-call(bf16[2,256,640]{2,1,0:T(8,128)(2,1)S(1)} %get-tuple-element.9.tokens_v, f32[16,640]{1,0:T(8,128)S(1)} %get-tuple-element.10.router_v, bf16[1280,1280]{1,0:T(8,128)(2,1)S(1)} %get-tuple-element.11.w_v), custom_call_target="tpu_custom_call" | custom-call | tf_op jit(solution)/shard_map/pallas_call | solution.py:293

commit v4 on v3

--- a/solution.py
+++ b/solution.py
@@ -11,7 +11,8 @@
 BF16 = jnp.bfloat16
 MESH = pl.DeviceIdType.MESH
 
-LOGITS, SLOTS, GRADS, OUT, IN, LOGIT_GRAD, SCATTER, GATHER = range(8)
+SLOTS, GRADS, OUT, IN, SCATTER, GATHER = range(6)
+SINGLE = 6
 
 
 def nt(a, b):
@@ -62,8 +63,11 @@
 
     barrier = pltpu.get_barrier_semaphore()
 
+    low = ep < n_ep // 2
+
     def wrapped(off):
-        to = ep + off
+        to = jnp.where(low, ep - off, ep + off)
+        to = jnp.where(to < 0, to + n_ep, to)
         return jnp.where(to >= n_ep, to - n_ep, to)
 
     def others(act):
@@ -88,26 +92,31 @@
             device_id=(ep, other), device_id_type=MESH,
         )
 
-    def send_all(src, by_expert, dst, k):
-        def send(to_ep, to_tp):
-            pltpu.make_async_remote_copy(
-                src_ref=src.at[to_ep if by_expert else to_tp * n_ep + to_ep], dst_ref=dst.at[me],
-                send_sem=send_sem.at[k], recv_sem=recv_sem.at[k],
-                device_id=(to_ep, to_tp), device_id_type=MESH,
-            ).start()
-
-        others(lambda to_ep: (send(to_ep, tp), send(to_ep, other)))
-        send(ep, other)
+    def send(src, dst, k, to_ep, to_tp):
+        pltpu.make_async_remote_copy(
+            src_ref=src, dst_ref=dst.at[me],
+            send_sem=send_sem.at[k], recv_sem=recv_sem.at[k],
+            device_id=(to_ep, to_tp), device_id_type=MESH,
+        ).start()
+
+    def send_all(src, dst, k):
+        others(
+            lambda to_ep: (
+                send(src.at[to_ep], dst, k, to_ep, tp),
+                send(src.at[to_ep], dst, k, to_ep, other),
+            )
+        )
+        send(src.at[ep], dst, k, ep, other)
 
     def send_row(src, dst, k):
-        def send(to_ep):
+        def send_one(to_ep):
             pltpu.make_async_remote_copy(
                 src_ref=src(to_ep), dst_ref=dst.at[ep],
                 send_sem=send_sem.at[k], recv_sem=recv_sem.at[k],
                 device_id=(to_ep, tp), device_id_type=MESH,
             ).start()
 
-        others(send)
+        others(send_one)
 
     def wait_blocks(ref, count, sem):
         blocks = ref.at[pl.ds(0, count)]
@@ -116,30 +125,30 @@
     loads[0].wait()
     loads[1].wait()
     router_t = router[...]
-    tok_rows = tok[...].reshape(images * patches, width)
-    logits_s[...] = nt(router_t, tok_rows)
+    for b in range(images):
+        logits_s[b] = nt(router_t, tok[b])
     pl.semaphore_wait(barrier, n_all - 1)
-    swap = to_partner(logits_s, logits_r, LOGITS)
-    swap.start()
-    swap.wait()
-    logits = logits_s[...] + logits_r[...]
-
-    def per_image(x):
-        return [x[:, b * patches : (b + 1) * patches] for b in range(images)]
+    swaps = [to_partner(logits_s.at[b], logits_r.at[b], SINGLE + b) for b in range(images)]
+    for swap in swaps:
+        swap.start()
 
     def softmax(x, axis):
         e = jnp.exp(x - jnp.max(x, axis=axis, keepdims=True))
         return e / jnp.sum(e, axis=axis, keepdims=True)
 
-    dispatch = [softmax(x, 1) for x in per_image(logits)]
-    combine = [softmax(x, 0) for x in per_image(logits)]
+    dispatch, combine = [], []
+    for b in range(images):
+        swaps[b].wait()
+        logits = logits_s[b] + logits_r[b]
+        dispatch.append(softmax(logits, 1))
+        combine.append(softmax(logits, 0))
     dispatch_b = [x.astype(BF16) for x in dispatch]
 
     def halves(weights, rows_of, ref_s, ref_r, k):
         parts = [nn(weights[b], rows_of[b]) for b in range(images)]
         ref_s[...] = jnp.stack(parts, axis=1).astype(BF16)
         ref_r[me] = ref_s[ep]
-        send_all(ref_s, True, ref_r, k)
+        send_all(ref_s, ref_r, k)
 
     halves(dispatch_b, tok, slots_s, slots_r, SLOTS)
     loads[2].wait()
@@ -155,21 +164,20 @@
     loads[4].wait()
     arrived(slots_r, slot_in, SLOTS)
 
-    def pieces(part, ref):
+    def send_back(half_of, src, dst, k):
         for s in range(2):
-            cut = part[:, s * width : (s + 1) * width]
-            ref[s * n_ep : (s + 1) * n_ep] = cut.reshape(n_ep, images, width).astype(BF16)
-
-    pre = nn(slot_in[...], w_in[...])
-    act, slope = gelu_parts(pre)
-    pieces(nn(act.astype(BF16), w_out[...]), out_s)
-    out_r[me] = out_s[me]
-    send_all(out_s, False, out_r, OUT)
+            part = half_of(slice(s * width, (s + 1) * width))
+            src[s * n_ep : (s + 1) * n_ep] = part.reshape(n_ep, images, width).astype(BF16)
+            others(lambda to_ep: send(src.at[s * n_ep + to_ep], dst, k, to_ep, s))
+        send(src.at[other * n_ep + ep], dst, k, ep, other)
+        dst[me] = src[me]
+
+    act, slope = gelu_parts(nn(slot_in[...], w_in[...]))
+    act = act.astype(BF16)
+    send_back(lambda cols: nn(act, w_out[:, cols]), out_s, out_r, OUT)
     arrived(grads_r, slot_grad, GRADS)
     pre_grad[...] = (slope * nt(slot_grad[...], w_out[...])).astype(BF16)
-    pieces(nt(pre_grad[...], w_in[...]), in_s)
-    in_r[me] = in_s[me]
-    send_all(in_s, False, in_r, IN)
+    send_back(lambda cols: nt(pre_grad[...], w_in[cols, :]), in_s, in_r, IN)
 
     tile = 256 if grad_w_o.shape[0] % 256 == 0 else 128
 
@@ -192,22 +200,26 @@
         shares.append(combine[b] * (dot - jnp.sum(combine[b] * dot, axis=0, keepdims=True)))
     wait_blocks(in_r, n_all - 1, recv_sem.at[IN])
     slot_in_grad = both_halves(in_r)
+    swaps = []
     for b in range(images):
         dot = nt(slot_in_grad[b], tok[b])
-        shares[b] += dispatch[b] * (dot - jnp.sum(dispatch[b] * dot, axis=1, keepdims=True))
-        lg_s[:, b * patches : (b + 1) * patches] = shares[b]
-    swap_lg = to_partner(lg_s, lg_r, LOGIT_GRAD)
-    swap_lg.start()
-    swap_lg.wait()
-    logit_b = (lg_s[...] + lg_r[...]).astype(BF16)
-
-    part = nn(logit_b, tok_rows)
+        lg_s[b] = shares[b] + dispatch[b] * (
+            dot - jnp.sum(dispatch[b] * dot, axis=1, keepdims=True)
+        )
+        swaps.append(to_partner(lg_s.at[b], lg_r.at[b], SINGLE + images + b))
+        swaps[b].start()
+    logit_b, part = [], 0.0
+    for b in range(images):
+        swaps[b].wait()
+        logit_b.append((lg_s[b] + lg_r[b]).astype(BF16))
+        part += nn(logit_b[b], tok[b])
+
     rs_s[...] = part.reshape(n_ep, experts // n_ep, width)
     rs_r[ep] = rs_s[ep]
     send_row(lambda to_ep: rs_s.at[to_ep], rs_r, SCATTER)
 
     def tokens_of(b):
-        left = jnp.concatenate([dispatch_b[b], per_image(logit_b)[b]], axis=0)
+        left = jnp.concatenate([dispatch_b[b], logit_b[b]], axis=0)
         right = jnp.concatenate([slot_in_grad[b], router_t], axis=0)
         grad_tokens_o[b] = tn(left, right).astype(BF16)
 
@@ -263,8 +275,8 @@
             vmem(w_in.shape, BF16),
             vmem(w_out.shape, BF16),
             vmem(grad_out.shape, BF16),
-            vmem((experts, images * patches), F32),
-            vmem((experts, images * patches), F32),
+            vmem((images, experts, patches), F32),
+            vmem((images, experts, patches), F32),
             vmem((experts, images, width), BF16),
             vmem((n_all, images, width), BF16),
             vmem((experts, images, width), BF16),
@@ -276,14 +288,14 @@
             vmem((n_all, images, width), BF16),
             vmem((n_all, images, width), BF16),
             vmem((n_all, images, width), BF16),
-            vmem((experts, images * patches), F32),
-            vmem((experts, images * patches), F32),
+            vmem((images, experts, patches), F32),
+            vmem((images, experts, patches), F32),
             vmem((n_ep, experts // n_ep, width), F32),
             vmem((n_ep, experts // n_ep, width), F32),
             vmem((n_ep, experts // n_ep, width), F32),
             pltpu.SemaphoreType.DMA((5,)),
-            pltpu.SemaphoreType.DMA((8,)),
-            pltpu.SemaphoreType.DMA((8,)),
+            pltpu.SemaphoreType.DMA((SINGLE + 2 * images,)),
+            pltpu.SemaphoreType.DMA((SINGLE + 2 * images,)),
         ],
         compiler_params=pltpu.CompilerParams(
             collective_id=0, has_side_effects=True, vmem_limit_bytes=40 * 1024 * 1024

time: 38 us -> 37.9 us (level)
  no operation moved by 1% of the time
where the time goes in v4:
time: 37.9 us; the launch traced here: 37.7 us
  Pallas kernels  37.1 us (98%)
  between operations  0.64 us (2%)
    pallas_call x1, Pallas kernels, on_device(): pl.pallas_call(functools.partial(kernel, n_ep), out_shape=(pltpu.VMEM(tok...  35.1 us
    pallas_call x1, Pallas kernels, on_device(): pl.pallas_call(write_out, out_shape=tuple((jax.ShapeDtypeStruct(x.shape,...  1.97 us

profile of v4, /device:TPU:0, one launch (start us, length us, event | category | flops | bytes accessed | tf_op | source)
XLA Modules:
  0.0 37.7 jit_solution(3759851060899086965)
XLA Ops:
  0.6 35.1 %shard_map.76 = (bf16[2,256,640]{2,1,0:T(8,128)(2,1)S(1)}, f32[16,640]{1,0:T(8,128)S(1)}, bf16[1280,1280]{1,0:T(8,128)(2,1)S(1)}) custom-call(bf16[2,256,640]{2,1,0:T(8,128)(2,1)} %tok_h.1, bf16[16,640]{1,0:T(8,128)(2,1)} %bitcast.7, bf16[1280,1280]{1,0:T(8,128)(2,1)} %bitcast.5, bf16[1280,1280]{1,0:T(8,128)(2,1)} %bitcast.6, bf16[2,256,640]{2,1,0:T(8,128)(2,1)} %grad_h.1), custom_call_target="tpu_custom_call" | custom-call | tf_op jit(solution)/shard_map/pallas_call | solution.py:263
  35.7 2.0 %shard_map.77 = (bf16[2,256,640]{2,1,0:T(8,128)(2,1)}, f32[16,640]{1,0:T(8,128)}, bf16[1280,1280]{1,0:T(8,128)(2,1)}) custom-call(bf16[2,256,640]{2,1,0:T(8,128)(2,1)S(1)} %get-tuple-element.9.tokens_v, f32[16,640]{1,0:T(8,128)S(1)} %get-tuple-element.10.router_v, bf16[1280,1280]{1,0:T(8,128)(2,1)S(1)} %get-tuple-element.11.w_v), custom_call_target="tpu_custom_call" | custom-call | tf_op jit(solution)/shard_map/pallas_call | solution.py:305

commit v5 on v4

--- a/solution.py
+++ b/solution.py
@@ -11,8 +11,8 @@
 BF16 = jnp.bfloat16
 MESH = pl.DeviceIdType.MESH
 
-SLOTS, GRADS, OUT, IN, SCATTER, GATHER = range(6)
-SINGLE = 6
+SLOTS, GRADS, BACK, SCATTER, GATHER = range(5)
+SINGLE = 5
 
 
 def nt(a, b):
@@ -41,7 +41,7 @@
     grad_tokens_o, grad_router_o, grad_w_o,
     tok, router, w_in, w_out, grad,
     logits_s, logits_r, slots_s, slots_r, grads_s, grads_r, slot_in, slot_grad, pre_grad,
-    out_s, out_r, in_s, in_r, lg_s, lg_r, rs_s, rs_r, ag,
+    back_s, back_r, lg_s, lg_r, rs_s, rs_r, ag,
     load_sem, send_sem, recv_sem,
 ):
     ep, tp = lax.axis_index("ep"), lax.axis_index("tp")
@@ -164,20 +164,21 @@
     loads[4].wait()
     arrived(slots_r, slot_in, SLOTS)
 
-    def send_back(half_of, src, dst, k):
-        for s in range(2):
-            part = half_of(slice(s * width, (s + 1) * width))
-            src[s * n_ep : (s + 1) * n_ep] = part.reshape(n_ep, images, width).astype(BF16)
-            others(lambda to_ep: send(src.at[s * n_ep + to_ep], dst, k, to_ep, s))
-        send(src.at[other * n_ep + ep], dst, k, ep, other)
-        dst[me] = src[me]
-
     act, slope = gelu_parts(nn(slot_in[...], w_in[...]))
-    act = act.astype(BF16)
-    send_back(lambda cols: nn(act, w_out[:, cols]), out_s, out_r, OUT)
     arrived(grads_r, slot_grad, GRADS)
     pre_grad[...] = (slope * nt(slot_grad[...], w_out[...])).astype(BF16)
-    send_back(lambda cols: nt(pre_grad[...], w_in[cols, :]), in_s, in_r, IN)
+    parts = (nt(pre_grad[...], w_in[...]), nn(act.astype(BF16), w_out[...]))
+    for s in range(2):
+        cut = [x[:, s * width : (s + 1) * width].reshape(n_ep, images, width) for x in parts]
+        back_s[s * n_ep : (s + 1) * n_ep] = jnp.concatenate(cut, axis=1).astype(BF16)
+    back_r[me] = back_s[me]
+    others(
+        lambda to_ep: (
+            send(back_s.at[tp * n_ep + to_ep], back_r, BACK, to_ep, tp),
+            send(back_s.at[other * n_ep + to_ep], back_r, BACK, to_ep, other),
+        )
+    )
+    send(back_s.at[other * n_ep + ep], back_r, BACK, ep, other)
 
     tile = 256 if grad_w_o.shape[0] % 256 == 0 else 128
 
@@ -188,22 +189,16 @@
 
     lax.fori_loop(0, grad_w_o.shape[0] // tile, grad_w_tile, 0)
 
-    def both_halves(ref):
-        total = ref[:n_ep].astype(F32) + ref[n_ep:].astype(F32)
-        return [total[:, b, :].astype(BF16) for b in range(images)]
-
-    wait_blocks(out_r, n_all - 1, recv_sem.at[OUT])
-    slot_out = both_halves(out_r)
-    shares = []
+    wait_blocks(back_r, n_all - 1, recv_sem.at[BACK])
+    total = back_r[:n_ep].astype(F32) + back_r[n_ep:].astype(F32)
+    slot_in_grad = [total[:, b, :].astype(BF16) for b in range(images)]
+    slot_out = [total[:, images + b, :].astype(BF16) for b in range(images)]
+    swaps = []
     for b in range(images):
         dot = nt(slot_out[b], grad[b])
-        shares.append(combine[b] * (dot - jnp.sum(combine[b] * dot, axis=0, keepdims=True)))
-    wait_blocks(in_r, n_all - 1, recv_sem.at[IN])
-    slot_in_grad = both_halves(in_r)
-    swaps = []
-    for b in range(images):
+        share = combine[b] * (dot - jnp.sum(combine[b] * dot, axis=0, keepdims=True))
         dot = nt(slot_in_grad[b], tok[b])
-        lg_s[b] = shares[b] + dispatch[b] * (
+        lg_s[b] = share + dispatch[b] * (
             dot - jnp.sum(dispatch[b] * dot, axis=1, keepdims=True)
         )
         swaps.append(to_partner(lg_s.at[b], lg_r.at[b], SINGLE + images + b))
@@ -235,8 +230,7 @@
 
     wait_blocks(slots_r, n_all - 1, send_sem.at[SLOTS])
     wait_blocks(grads_r, n_all - 1, send_sem.at[GRADS])
-    wait_blocks(out_r, n_all - 1, send_sem.at[OUT])
-    wait_blocks(in_r, n_all - 1, send_sem.at[IN])
+    wait_blocks(back_r, n_all - 1, send_sem.at[BACK])
     wait_blocks(rs_r, n_ep - 1, send_sem.at[SCATTER])
     wait_blocks(ag, n_ep - 1, send_sem.at[GATHER])
 
@@ -284,10 +278,8 @@
             vmem((rows, model), BF16),
             vmem((rows, model), BF16),
             vmem((rows, hidden), BF16),
-            vmem((n_all, images, width), BF16),
-            vmem((n_all, images, width), BF16),
-            vmem((n_all, images, width), BF16),
-            vmem((n_all, images, width), BF16),
+            vmem((n_all, 2 * images, width), BF16),
+            vmem((n_all, 2 * images, width), BF16),
             vmem((images, experts, patches), F32),
             vmem((images, experts, patches), F32),
             vmem((n_ep, experts // n_ep, width), F32),

time: 37.9 us -> 38.2 us (level)
  no operation moved by 1% of the time
where the time goes in v5:
time: 38.2 us; the launch traced here: 38.1 us
  Pallas kernels  37.4 us (98%)
  between operations  0.64 us (2%)
    pallas_call x1, Pallas kernels, on_device(): pl.pallas_call(functools.partial(kernel, n_ep), out_shape=(pltpu.VMEM(tok...  35.4 us
    pallas_call x1, Pallas kernels, on_device(): pl.pallas_call(write_out, out_shape=tuple((jax.ShapeDtypeStruct(x.shape,...  1.97 us

profile of v5, /device:TPU:0, one launch (start us, length us, event | category | flops | bytes accessed | tf_op | source)
XLA Modules:
  0.0 38.1 jit_solution(9195760917599725028)
XLA Ops:
  0.6 35.4 %shard_map.76 = (bf16[2,256,640]{2,1,0:T(8,128)(2,1)S(1)}, f32[16,640]{1,0:T(8,128)S(1)}, bf16[1280,1280]{1,0:T(8,128)(2,1)S(1)}) custom-call(bf16[2,256,640]{2,1,0:T(8,128)(2,1)} %tok_h.1, bf16[16,640]{1,0:T(8,128)(2,1)} %bitcast.7, bf16[1280,1280]{1,0:T(8,128)(2,1)} %bitcast.5, bf16[1280,1280]{1,0:T(8,128)(2,1)} %bitcast.6, bf16[2,256,640]{2,1,0:T(8,128)(2,1)} %grad_h.1), custom_call_target="tpu_custom_call" | custom-call | tf_op jit(solution)/shard_map/pallas_call | solution.py:257
  36.1 2.0 %shard_map.77 = (bf16[2,256,640]{2,1,0:T(8,128)(2,1)}, f32[16,640]{1,0:T(8,128)}, bf16[1280,1280]{1,0:T(8,128)(2,1)}) custom-call(bf16[2,256,640]{2,1,0:T(8,128)(2,1)S(1)} %get-tuple-element.9.tokens_v, f32[16,640]{1,0:T(8,128)S(1)} %get-tuple-element.10.router_v, bf16[1280,1280]{1,0:T(8,128)(2,1)S(1)} %get-tuple-element.11.w_v), custom_call_target="tpu_custom_call" | custom-call | tf_op jit(solution)/shard_map/pallas_call | solution.py:297

commit v6 on v4

--- a/solution.py
+++ b/solution.py
@@ -11,8 +11,7 @@
 BF16 = jnp.bfloat16
 MESH = pl.DeviceIdType.MESH
 
-SLOTS, GRADS, OUT, IN, SCATTER, GATHER = range(6)
-SINGLE = 6
+SLOTS, GRADS, OUT, IN, SCATTER, GATHER, SINGLE = 0, 2, 3, 4, 5, 6, 7
 
 
 def nt(a, b):
@@ -58,8 +57,8 @@
             ((tok_h, tok), (router_h, router), (grad_h, grad), (w_in_h, w_in), (w_out_h, w_out))
         )
     ]
-    for load in loads:
-        load.start()
+    loads[0].start()
+    loads[1].start()
 
     barrier = pltpu.get_barrier_semaphore()
 
@@ -85,6 +84,8 @@
 
     greet(ep, other)
     others(lambda to_ep: (greet(to_ep, tp), greet(to_ep, other)))
+    for load in loads[2:]:
+        load.start()
 
     def to_partner(src, dst, k):
         return pltpu.make_async_remote_copy(
@@ -136,23 +137,26 @@
         e = jnp.exp(x - jnp.max(x, axis=axis, keepdims=True))
         return e / jnp.sum(e, axis=axis, keepdims=True)
 
-    dispatch, combine = [], []
+    dispatch, logits = [], []
     for b in range(images):
         swaps[b].wait()
-        logits = logits_s[b] + logits_r[b]
-        dispatch.append(softmax(logits, 1))
-        combine.append(softmax(logits, 0))
+        logits.append(logits_s[b] + logits_r[b])
+        dispatch.append(softmax(logits[b], 1))
     dispatch_b = [x.astype(BF16) for x in dispatch]
 
-    def halves(weights, rows_of, ref_s, ref_r, k):
+    def halves(weights, rows_of, ref_s, ref_r):
         parts = [nn(weights[b], rows_of[b]) for b in range(images)]
         ref_s[...] = jnp.stack(parts, axis=1).astype(BF16)
         ref_r[me] = ref_s[ep]
-        send_all(ref_s, ref_r, k)
-
-    halves(dispatch_b, tok, slots_s, slots_r, SLOTS)
+
+    halves(dispatch_b, tok, slots_s, slots_r)
+    others(lambda to_ep: send(slots_s.at[to_ep], slots_r, SLOTS + tp, to_ep, tp))
+    others(lambda to_ep: send(slots_s.at[to_ep], slots_r, SLOTS + tp, to_ep, other))
+    send(slots_s.at[ep], slots_r, SLOTS + tp, ep, other)
+    combine = [softmax(x, 0) for x in logits]
     loads[2].wait()
-    halves([x.astype(BF16) for x in combine], grad, grads_s, grads_r, GRADS)
+    halves([x.astype(BF16) for x in combine], grad, grads_s, grads_r)
+    send_all(grads_s, grads_r, GRADS)
 
     def arrived(ref, dst, k):
         wait_blocks(ref, n_all - 1, recv_sem.at[k])
@@ -162,7 +166,13 @@
 
     loads[3].wait()
     loads[4].wait()
-    arrived(slots_r, slot_in, SLOTS)
+    pre = 0.0
+    for s, count in ((tp, n_ep - 1), (other, n_ep)):
+        wait_blocks(slots_r, count, recv_sem.at[SLOTS + s])
+        half = slots_r[pl.ds(s * n_ep, n_ep)].astype(F32).reshape(rows, width).astype(BF16)
+        at = pl.ds(pl.multiple_of(s * width, 128), width)
+        slot_in[:, at] = half
+        pre += nn(half, w_in[at, :])
 
     def send_back(half_of, src, dst, k):
         for s in range(2):
@@ -172,7 +182,7 @@
         send(src.at[other * n_ep + ep], dst, k, ep, other)
         dst[me] = src[me]
 
-    act, slope = gelu_parts(nn(slot_in[...], w_in[...]))
+    act, slope = gelu_parts(pre)
     act = act.astype(BF16)
     send_back(lambda cols: nn(act, w_out[:, cols]), out_s, out_r, OUT)
     arrived(grads_r, slot_grad, GRADS)
@@ -233,7 +243,7 @@
     wait_blocks(ag, n_ep - 1, recv_sem.at[GATHER])
     grad_router_o[...] = ag[...].reshape(experts, width)
 
-    wait_blocks(slots_r, n_all - 1, send_sem.at[SLOTS])
+    wait_blocks(slots_r, n_all - 1, send_sem.at[SLOTS + tp])
     wait_blocks(grads_r, n_all - 1, send_sem.at[GRADS])
     wait_blocks(out_r, n_all - 1, send_sem.at[OUT])
     wait_blocks(in_r, n_all - 1, send_sem.at[IN])

time: 37.9 us -> 38.1 us (level)
  no operation moved by 1% of the time
where the time goes in v6:
time: 38.1 us; the launch traced here: 38 us
  Pallas kernels  37.3 us (98%)
  between operations  0.64 us (2%)
    pallas_call x1, Pallas kernels, on_device(): pl.pallas_call(functools.partial(kernel, n_ep), out_shape=(pltpu.VMEM(tok...  35.3 us
    pallas_call x1, Pallas kernels, on_device(): pl.pallas_call(write_out, out_shape=tuple((jax.ShapeDtypeStruct(x.shape,...  1.97 us

profile of v6, /device:TPU:0, one launch (start us, length us, event | category | flops | bytes accessed | tf_op | source)
XLA Modules:
  0.0 38.0 jit_solution(10075952618310903154)
XLA Ops:
  0.6 35.3 %shard_map.76 = (bf16[2,256,640]{2,1,0:T(8,128)(2,1)S(1)}, f32[16,640]{1,0:T(8,128)S(1)}, bf16[1280,1280]{1,0:T(8,128)(2,1)S(1)}) custom-call(bf16[2,256,640]{2,1,0:T(8,128)(2,1)} %tok_h.1, bf16[16,640]{1,0:T(8,128)(2,1)} %bitcast.7, bf16[1280,1280]{1,0:T(8,128)(2,1)} %bitcast.5, bf16[1280,1280]{1,0:T(8,128)(2,1)} %bitcast.6, bf16[2,256,640]{2,1,0:T(8,128)(2,1)} %grad_h.1), custom_call_target="tpu_custom_call" | custom-call | tf_op jit(solution)/shard_map/pallas_call | solution.py:273
  36.0 2.0 %shard_map.77 = (bf16[2,256,640]{2,1,0:T(8,128)(2,1)}, f32[16,640]{1,0:T(8,128)}, bf16[1280,1280]{1,0:T(8,128)(2,1)}) custom-call(bf16[2,256,640]{2,1,0:T(8,128)(2,1)S(1)} %get-tuple-element.9.tokens_v, f32[16,640]{1,0:T(8,128)S(1)} %get-tuple-element.10.router_v, bf16[1280,1280]{1,0:T(8,128)(2,1)S(1)} %get-tuple-element.11.w_v), custom_call_target="tpu_custom_call" | custom-call | tf_op jit(solution)/shard_map/pallas_call | solution.py:315

commit v7 on v4

--- a/solution.py
+++ b/solution.py
@@ -40,7 +40,7 @@
     tok_h, router_h, w_in_h, w_out_h, grad_h,
     grad_tokens_o, grad_router_o, grad_w_o,
     tok, router, w_in, w_out, grad,
-    logits_s, logits_r, slots_s, slots_r, grads_s, grads_r, slot_in, slot_grad, pre_grad,
+    logits_s, logits_r, slots_s, slots_r, grads_s, grads_r, slot_in, slot_grad, pre_grad, act, slope, part,
     out_s, out_r, in_s, in_r, lg_s, lg_r, rs_s, rs_r, ag,
     load_sem, send_sem, recv_sem,
 ):
@@ -164,6 +164,16 @@
     loads[4].wait()
     arrived(slots_r, slot_in, SLOTS)
 
+    hidden = w_in.shape[1]
+    step = 256 if hidden % 256 == 0 else 128
+
+    def tiles(size, body):
+        def one(i, carry):
+            body(pl.ds(pl.multiple_of(i * step, step), step))
+            return carry
+
+        lax.fori_loop(0, size // step, one, 0)
+
     def send_back(half_of, src, dst, k):
         for s in range(2):
             part = half_of(slice(s * width, (s + 1) * width))
@@ -172,12 +182,28 @@
         send(src.at[other * n_ep + ep], dst, k, ep, other)
         dst[me] = src[me]
 
-    act, slope = gelu_parts(nn(slot_in[...], w_in[...]))
-    act = act.astype(BF16)
-    send_back(lambda cols: nn(act, w_out[:, cols]), out_s, out_r, OUT)
+    def first(cols):
+        act[:, cols], slope[:, cols] = (
+            lambda a, g: (a.astype(BF16), g)
+        )(*gelu_parts(nn(slot_in[...], w_in[:, cols])))
+
+    def second(cols):
+        part[:, cols] = nn(act[...], w_out[:, cols])
+
+    def third(cols):
+        back = nt(slot_grad[...], w_out[cols, :])
+        pre_grad[:, cols] = (slope[:, cols] * back).astype(BF16)
+
+    def fourth(cols):
+        part[:, cols] = nt(pre_grad[...], w_in[cols, :])
+
+    tiles(hidden, first)
+    tiles(2 * width, second)
+    send_back(lambda cols: part[:, cols], out_s, out_r, OUT)
     arrived(grads_r, slot_grad, GRADS)
-    pre_grad[...] = (slope * nt(slot_grad[...], w_out[...])).astype(BF16)
-    send_back(lambda cols: nt(pre_grad[...], w_in[cols, :]), in_s, in_r, IN)
+    tiles(hidden, third)
+    tiles(2 * width, fourth)
+    send_back(lambda cols: part[:, cols], in_s, in_r, IN)
 
     tile = 256 if grad_w_o.shape[0] % 256 == 0 else 128
 
@@ -208,13 +234,13 @@
         )
         swaps.append(to_partner(lg_s.at[b], lg_r.at[b], SINGLE + images + b))
         swaps[b].start()
-    logit_b, part = [], 0.0
+    logit_b, share = [], 0.0
     for b in range(images):
         swaps[b].wait()
         logit_b.append((lg_s[b] + lg_r[b]).astype(BF16))
-        part += nn(logit_b[b], tok[b])
-
-    rs_s[...] = part.reshape(n_ep, experts // n_ep, width)
+        share += nn(logit_b[b], tok[b])
+
+    rs_s[...] = share.reshape(n_ep, experts // n_ep, width)
     rs_r[ep] = rs_s[ep]
     send_row(lambda to_ep: rs_s.at[to_ep], rs_r, SCATTER)
 
@@ -284,6 +310,9 @@
             vmem((rows, model), BF16),
             vmem((rows, model), BF16),
             vmem((rows, hidden), BF16),
+            vmem((rows, hidden), BF16),
+            vmem((rows, hidden), F32),
+            vmem((rows, model), F32),
             vmem((n_all, images, width), BF16),
             vmem((n_all, images, width), BF16),
             vmem((n_all, images, width), BF16),

time: 37.9 us -> 40.4 us (1.066)
  Pallas kernels: 37.1 us -> 39.6 us
    pallas_call x1, Pallas kernels: 35.1 us -> 37.6 us  [on_device(): pl.pallas_call(functools.partial(kernel, n_ep), out_shape=(pltpu.VMEM(tok...]
where the time goes in v7:
time: 40.4 us; the launch traced here: 40.3 us
  Pallas kernels  39.6 us (98%)
  between operations  0.64 us (2%)
    pallas_call x1, Pallas kernels, on_device(): pl.pallas_call(functools.partial(kernel, n_ep), out_shape=(pltpu.VMEM(tok...  37.6 us
    pallas_call x1, Pallas kernels, on_device(): pl.pallas_call(write_out, out_shape=tuple((jax.ShapeDtypeStruct(x.shape,...  1.97 us

profile of v7, /device:TPU:0, one launch (start us, length us, event | category | flops | bytes accessed | tf_op | source)
XLA Modules:
  0.0 40.3 jit_solution(11458815598752647688)
XLA Ops:
  0.6 37.6 %shard_map.76 = (bf16[2,256,640]{2,1,0:T(8,128)(2,1)S(1)}, f32[16,640]{1,0:T(8,128)S(1)}, bf16[1280,1280]{1,0:T(8,128)(2,1)S(1)}) custom-call(bf16[2,256,640]{2,1,0:T(8,128)(2,1)} %tok_h.1, bf16[16,640]{1,0:T(8,128)(2,1)} %bitcast.7, bf16[1280,1280]{1,0:T(8,128)(2,1)} %bitcast.5, bf16[1280,1280]{1,0:T(8,128)(2,1)} %bitcast.6, bf16[2,256,640]{2,1,0:T(8,128)(2,1)} %grad_h.1), custom_call_target="tpu_custom_call" | custom-call | tf_op jit(solution)/shard_map/pallas_call | solution.py:289
  38.3 2.0 %shard_map.77 = (bf16[2,256,640]{2,1,0:T(8,128)(2,1)}, f32[16,640]{1,0:T(8,128)}, bf16[1280,1280]{1,0:T(8,128)(2,1)}) custom-call(bf16[2,256,640]{2,1,0:T(8,128)(2,1)S(1)} %get-tuple-element.9.tokens_v, f32[16,640]{1,0:T(8,128)S(1)} %get-tuple-element.10.router_v, bf16[1280,1280]{1,0:T(8,128)(2,1)S(1)} %get-tuple-element.11.w_v), custom_call_target="tpu_custom_call" | custom-call | tf_op jit(solution)/shard_map/pallas_call | solution.py:334
